TPU v7x, 32 devices: a whole 2x2x4 slice. The times are simulated.
32 devices in a mesh: prow: 8 (over z, core), pcol: 4 (over y, x).
Axes of the slice: x: 2, y: 2, z: 4, core: 2. Of those that a mesh axis runs over, the one named last changes fastest.
Arguments:
- kernel: float32 [6, 8, 256, 12, 4, 256], P(None, 'prow', None, None, 'pcol'), as said below
Outputs:
- factored: float32 [6, 8, 256, 12, 4, 256], P(None, 'prow', None, None, 'pcol')
Inputs may be any that keep to these rules, and one draw needn't show every extreme that they name: kernel is symmetric (entry (a, b) equals entry (b, a)); every diagonal entry is 1.1, every off-diagonal entry lies in (0, 1], and the matrix is positive definite with smallest eigenvalue at least 0.1.
All inputs are finite; a program needn't handle non-finite values.
Results may differ from a plain program's by a relative error of at most 0.0003.
Values sent between devices are 32-bit elements; how exact they have to be, the bound alone decides.
A program may use at most 128 MiB of HBM per device.

v0:
```python
import jax
import jax.numpy as jnp
from jax import lax
from jax.sharding import PartitionSpec as P

STEPS = 2


def picked_rows(trailing, rows, prow_idx, col_ids):
    source = col_ids // rows
    owner = col_ids % rows
    chosen = jnp.take(trailing, source, axis=0)
    masked = jnp.where((owner == prow_idx)[:, None, None], chosen, 0.0)
    return lax.psum(masked, "prow")


def on_device(kernel):
    rows = lax.axis_size("prow")
    cols = lax.axis_size("pcol")
    prow_idx = lax.axis_index("prow")
    pcol_idx = lax.axis_index("pcol")
    lbr, blk, lbc = (kernel.shape[0], kernel.shape[2], kernel.shape[3])
    work = kernel.reshape(lbr, blk, lbc, blk)
    row_ids = jnp.arange(lbr, dtype=jnp.int32) * rows + prow_idx
    col_ids = jnp.arange(lbc, dtype=jnp.int32) * cols + pcol_idx
    eye = jnp.eye(blk, dtype=jnp.float32)
    place = row_ids[:, None, None]

    def partner_rows(trailing):
        return picked_rows(trailing, rows, prow_idx, col_ids)

    def factor(matrix, k):
        candidate = matrix[k // rows, :, k // cols, :]
        candidate = jnp.where(prow_idx == k % rows, candidate, 0.0)
        block = lax.psum(candidate, "prow")
        block = jnp.where(pcol_idx == k % cols, block, eye)
        lower = jnp.linalg.cholesky(block)
        inverse = jax.scipy.linalg.solve_triangular(lower, eye, lower=True)
        column = matrix[:, :, k // cols, :]
        product = jnp.einsum("rib,jb->rij", column, inverse, precision=lax.Precision.HIGHEST)
        panel_out = jnp.where(place > k, product, jnp.where(place == k, lower[None], 0.0))
        masked = jnp.where(pcol_idx == k % cols, panel_out, 0.0)
        shared = lax.psum(masked, "pcol")
        trailing = jnp.where(place > k, shared, 0.0)
        return (panel_out, trailing, partner_rows(trailing))

    def update(matrix, factors, start, stop):
        if stop <= start:
            return matrix
        delta = jnp.einsum(
            "rib,cjb->ricj", factors[1], factors[2][start:stop], precision=lax.Precision.HIGHEST
        )
        return matrix.at[:, :, start:stop, :].set(matrix[:, :, start:stop, :] - delta)

    def write(matrix, factors, k):
        local_col = k // cols
        column = jnp.where(pcol_idx == k % cols, factors[0], matrix[:, :, local_col, :])
        matrix = matrix.at[:, :, local_col, :].set(column)
        upper = (row_ids == k)[:, None, None, None] & (col_ids > k)[None, None, :, None]
        return jnp.where(upper, 0.0, matrix)

    factors = factor(work, 0)
    for k in range(STEPS):
        if k + 1 < STEPS:
            nearby = (k + 1) // cols
            work = update(work, factors, nearby, nearby + 1)
            following = factor(work, k + 1)
            work = update(work, factors, 0, nearby)
            work = update(work, factors, nearby + 1, lbc)
            work = write(work, factors, k)
            factors = following
        else:
            work = update(work, factors, 0, lbc)
            work = write(work, factors, k)
    return work.reshape(kernel.shape)


def solution(mesh):
    in_specs = (P(None, "prow", None, None, "pcol", None),)
    out_specs = P(None, "prow", None, None, "pcol", None)
    return jax.shard_map(
        on_device, mesh=mesh, in_specs=in_specs, out_specs=out_specs, check_vma=False
    )
```

profile of v0, /device:TPU:29, one launch (start us, length us, event | category | flops | bytes accessed | tf_op | source)
XLA Modules:
  0.0 685.6 jit_solution(4906248022596451609)
XLA Ops:
  6.5 44.6 %copy.2 = f32[6,1,256,12,1,256]{2,5,3,0,4,1:T(8,128)} copy(f32[6,1,256,12,1,256]{5,4,3,2,1,0:T(1,128)} %param.18) | data formatting | bytes 37748736 | tf_op args[0]
  52.9 53.2 %all-reduce.8.cloned.1.call-done = f32[256,256]{0,1:T(8,128)} async-done(((f32[256,256]{0,1:T(8,128)}), f32[256,256]{0,1:T(8,128)}) %all-reduce.8.cloned.1.call-update) | async-done | bytes 262160 | tf_op jit(solution)/shard_map/psum | solution.py:35
  106.3 11.7 %cholesky.130 = f32[128,128]{1,0:T(8,128)S(1)} custom-call(f32[128,128]{1,0:T(8,128)S(1)} %cholesky.194), custom_call_target="Cholesky" | custom-call | tf_op jit(solution)/shard_map/jit(cholesky)/cholesky | solution.py:37
  118.1 9.8 %custom-call.13 = f32[1,128,128]{1,2,0:T(8,128)S(1)} custom-call(f32[1,128,128]{2,1,0:T(8,128)S(1)} %get-tuple-element.123), custom_call_target="InvertDiagBlocksLowerTriangular" | custom-call | tf_op jit(solution)/shard_map/jit(cholesky)/cholesky | solution.py:37
  128.4 11.7 %cholesky.147 = f32[128,128]{1,0:T(8,128)S(1)} custom-call(f32[128,128]{1,0:T(8,128)S(1)} %convolution_subtract_fusion.3), custom_call_target="Cholesky" | custom-call | tf_op jit(solution)/shard_map/jit(cholesky)/cholesky | solution.py:37
  142.3 4.1 while.10
  146.5 19.7 %custom-call.14 = f32[2,128,128]{1,2,0:T(8,128)S(1)} custom-call(f32[2,128,128]{2,1,0:T(8,128)S(1)} %get-tuple-element.90), custom_call_target="InvertDiagBlocksLowerTriangular" | custom-call | tf_op jit(solution)/shard_map/jit(_solve_triangular)/triangular_solve | solution.py:38
  167.2 4.6 broadcast_select_fusion.3
  172.0 62.6 %all-reduce.10.cloned.1.call-done = f32[6,256,256]{1,2,0:T(8,128)} async-done(((f32[6,256,256]{1,2,0:T(8,128)}), f32[6,256,256]{1,2,0:T(8,128)}) %all-reduce.10.cloned.1.call-update) | async-done | bytes 1572880 | tf_op jit(solution)/shard_map/psum | solution.py:43
  236.2 2.4 gather_fusion
  238.6 3.9 select_select_fusion.1
  242.7 76.2 %all-reduce.12.cloned.1.call-done = f32[12,256,256]{1,2,0:T(8,128)} async-done(((f32[12,256,256]{1,2,0:T(8,128)}), f32[12,256,256]{1,2,0:T(8,128)}) %all-reduce.12.cloned.1.call-update) | async-done | bytes 3145744 | tf_op jit(solution)/shard_map/psum | solution.py:14
  318.9 3.1 bitcast_subtract_fusion
  323.3 52.7 %all-reduce.14.cloned.1.call-done = f32[256,256]{0,1:T(8,128)} async-done(((f32[256,256]{0,1:T(8,128)}), f32[256,256]{0,1:T(8,128)}) %all-reduce.14.cloned.1.call-update) | async-done | bytes 262160 | tf_op jit(solution)/shard_map/psum | solution.py:35
  380.2 11.7 %cholesky.164 = f32[128,128]{1,0:T(8,128)S(1)} custom-call(f32[128,128]{1,0:T(8,128)S(1)} %cholesky.197), custom_call_target="Cholesky" | custom-call | tf_op jit(solution)/shard_map/jit(cholesky)/cholesky | solution.py:37
  393.2 9.8 %custom-call.15 = f32[1,128,128]{1,2,0:T(8,128)S(1)} custom-call(f32[1,128,128]{2,1,0:T(8,128)S(1)} %get-tuple-element.119), custom_call_target="InvertDiagBlocksLowerTriangular" | custom-call | tf_op jit(solution)/shard_map/jit(cholesky)/cholesky | solution.py:37
  405.7 11.7 %cholesky.181 = f32[128,128]{1,0:T(8,128)S(1)} custom-call(f32[128,128]{1,0:T(8,128)S(1)} %convolution_subtract_fusion.2), custom_call_target="Cholesky" | custom-call | tf_op jit(solution)/shard_map/jit(cholesky)/cholesky | solution.py:37
  425.0 7.2 %while.11 = (s32[]{:T(128)}, f32[256,256]{1,0:T(8,128)}, s32[2,2]{1,0:T(2,128)}, f32[2,128,128]{2,1,0:T(8,128)S(1)}, s32[]{:T(128)}) while((s32[]{:T(128)}, f32[256,256]{1,0:T(8,128)}, s32[2,2]{1,0:T(2,128)}, f32[2,128,128]{2,1,0:T(8,128)S(1)}, s32[]{:T(128)}) %tuple.90), condition=%wide.while_cond.5.clone, body=%wide.while_body.5.clone.sunk | while | flops 2 | bytes 131189 | solution.py:38
  426.5 2.2 bitcast_dynamic-update-slice_fusion.5
  430.0 2.2 bitcast_dynamic-update-slice_fusion.5
  432.9 20.5 %custom-call.16 = f32[2,128,128]{1,2,0:T(8,128)S(1)} custom-call(f32[2,128,128]{2,1,0:T(8,128)} %copy-done.5), custom_call_target="InvertDiagBlocksLowerTriangular" | custom-call | tf_op jit(solution)/shard_map/jit(_solve_triangular)/triangular_solve | solution.py:38
  455.2 4.3 broadcast_select_fusion.1
  459.8 62.5 %all-reduce.16.cloned.1.call-done = f32[6,256,256]{1,2,0:T(8,128)} async-done(((f32[6,256,256]{1,2,0:T(8,128)}), f32[6,256,256]{1,2,0:T(8,128)}) %all-reduce.16.cloned.1.call-update) | async-done | bytes 1572880 | tf_op jit(solution)/shard_map/psum | solution.py:43
  523.9 2.4 gather_fusion.1
  526.4 4.0 select_select_fusion
  530.4 2.9 constant_dynamic-update-slice_fusion.2
  533.3 19.9 %fusion = f32[6,256,12,256]{1,3,2,0:T(8,128)} fusion(f32[6,256,12,256]{1,3,2,0:T(8,128)} %constant_dynamic-update-slice_fusion.2, f32[12,256,256]{1,2,0:T(8,128)S(1)} %copy-done.3, f32[6,256,256]{1,2,0:T(8,128)S(1)} %broadcast_select_fusion.2), kind=kOutput, calls=%fused_computation.9 | convolution fusion | flops 13291880448 | bytes 39059456 | tf_op jit(solution)/shard_map/rib,cjb->ricj/dot_general | solution.py:50
  553.3 2.8 fusion.7
  556.0 50.6 %all-reduce.18.cloned.1.call-done = f32[12,256,256]{1,2,0:T(8,128)} async-done(((f32[12,256,256]{1,2,0:T(8,128)}), f32[12,256,256]{1,2,0:T(8,128)}) %all-reduce.18.cloned.1.call-update) | async-done | bytes 3145744 | tf_op jit(solution)/shard_map/psum | solution.py:14
  606.7 20.0 %select_subtract_fusion = f32[6,256,12,256]{1,3,2,0:T(8,128)S(1)} fusion(f32[6,256,12,256]{1,3,2,0:T(8,128)} %fusion.7, pred[6,12]{1,0:T(8,128)(4,1)S(1)} %broadcast_and_fusion, f32[12,256,256]{1,2,0:T(8,128)} %all-reduce.18.cloned.1.call-done, f32[6,256,256]{1,2,0:T(8,128)S(1)} %broadcast_select_fusion), kind=kOutput, calls=%fused_computation.7 | convolution fusion | flops 14504951808 | bytes 42467400 | tf_op jit(solution)/shard_map/rib,cjb->ricj/dot_general | solution.py:50
  627.0 7.0 %select_bitcast_fusion = f32[6,1,256,12,1,256]{2,5,3,0,4,1:T(8,128)} fusion(f32[6,256,12,256]{1,3,2,0:T(8,128)S(1)} %fusion.4, pred[6,12]{1,0:T(8,128)(4,1)S(1)} %broadcast_and_fusion.1), kind=kLoop, calls=%fused_computation.6 | loop fusion | flops 4718592 | bytes 37748808 | tf_op jit(solution)/shard_map/reshape | solution.py:75
  634.0 44.5 %copy.22 = f32[6,1,256,12,1,256]{5,4,3,2,1,0:T(1,128)} copy(f32[6,1,256,12,1,256]{2,5,3,0,4,1:T(8,128)} %select_bitcast_fusion) | data formatting | bytes 37748736 | tf_op jit(solution)/shard_map/reshape | solution.py:75
  (96 shorter events, 33.2 us)
Async XLA Ops:
  6.5 99.6 %all-reduce.8.cloned.1.call-start = ((), (), s32[]{:S(2)}) async-start(), calls=%async_computation | async-start | bytes 524288 | tf_op jit(solution)/shard_map/psum | solution.py:35
  52.8 181.8 %all-reduce.10.cloned.1.call-start = ((), (), s32[]{:S(2)}) async-start(), calls=%async_computation.1 | async-start | bytes 3145728 | tf_op jit(solution)/shard_map/psum | solution.py:43
  146.5 25.4 %copy-start.10 = (s32[2,2]{1,0:T(2,128)}, s32[2,2]{1,0:T(2,128)S(1)}, u32[]{:S(2)}) copy-start(s32[2,2]{1,0:T(2,128)S(1)} %get-tuple-element.250) | copy-start | bytes 52
  171.9 147.0 %all-reduce.12.cloned.1.call-start = ((), (), s32[]{:S(2)}) async-start(), calls=%async_computation.2 | async-start | bytes 6291456 | tf_op jit(solution)/shard_map/psum | solution.py:14
  172.0 66.7 %copy-start.6 = (pred[12]{0:T(512)(128)(4,1)}, pred[12]{0:T(512)(128)(4,1)S(1)}, u32[]{:S(2)}) copy-start(pred[12]{0:T(512)(128)(4,1)S(1)} %compare_and_fusion) | copy-start | bytes 40
  172.0 66.6 %copy-start.8 = (pred[12]{0:T(512)(128)(4,1)}, pred[12]{0:T(512)(128)(4,1)S(1)}, u32[]{:S(2)}) copy-start(pred[12]{0:T(512)(128)(4,1)S(1)} %fusion.47) | copy-start | bytes 40
  242.6 133.4 %all-reduce.14.cloned.1.call-start = ((), (), s32[]{:S(2)}) async-start(), calls=%async_computation.3 | async-start | bytes 524288 | tf_op jit(solution)/shard_map/psum | solution.py:35
  321.9 133.3 %copy-start = (f32[6,256,1,256]{1,3,2,0:T(8,128)}, f32[6,256,1,256]{1,3,2,0:T(8,128)S(1)}, u32[]{:S(2)}) copy-start(f32[6,256,1,256]{1,3,2,0:T(8,128)S(1)} %bitcast_subtract_fusion) | copy-start | bytes 4718596
  322.8 199.5 %all-reduce.16.cloned.1.call-start = ((), (), s32[]{:S(2)}) async-start(), calls=%async_computation.4 | async-start | bytes 3145728 | tf_op jit(solution)/shard_map/psum | solution.py:43
  379.5 0.7 copy-start.4
  432.2 0.7 copy-start.5
  459.5 147.1 %all-reduce.18.cloned.1.call-start = ((), (), s32[]{:S(2)}) async-start(), calls=%async_computation.5 | async-start | bytes 6291456 | tf_op jit(solution)/shard_map/psum | solution.py:14
  523.9 2.5 copy-start.7
  523.9 2.5 copy-start.9
  530.4 2.9 copy-start.3
  533.3 19.9 %copy-start.1 = (f32[6,256,256]{1,2,0:T(8,128)S(1)}, f32[6,256,256]{1,2,0:T(8,128)}, u32[]{:S(2)}) copy-start(f32[6,256,256]{1,2,0:T(8,128)} %get-tuple-element.127) | copy-start | bytes 4718596
  556.0 70.6 %copy-start.2 = (f32[6,256,256]{1,2,0:T(8,128)S(1)}, f32[6,256,256]{1,2,0:T(8,128)}, u32[]{:S(2)}) copy-start(f32[6,256,256]{1,2,0:T(8,128)} %get-tuple-element.131) | copy-start | bytes 4718596
Sparse Core Ops, SparseCore 0:
  52.9 53.1 all-reduce.7
  172.0 62.5 all-reduce.9
  242.7 76.0 all-reduce.11
  322.9 53.0 all-reduce.13
  459.7 62.5 all-reduce.15
  530.5 76.0 all-reduce.17
where the time goes:
time: 700 us; the launch traced here: 686 us
  waiting for transfers between devices  358 us (51%)
  other arithmetic  138 us (20%)
  local copies, waits for them, and re-layouts  114 us (16%)
  matrix products  58 us (8%)
  between operations  16.6 us (2%)
    psum x2, waiting for transfers between devices, picked_rows(): return lax.psum(masked, 'prow')  127 us
    psum x2, waiting for transfers between devices, factor(): shared = lax.psum(masked, 'pcol')  125 us
    psum x2, waiting for transfers between devices, factor(): block = lax.psum(candidate, 'prow')  106 us
    another operation x13, other arithmetic, factor(): lower = jnp.linalg.cholesky(block)  70.4 us
    unnamed x23, local copies, waits for them, and re-layouts  45.9 us
    reshape x1, local copies, waits for them, and re-layouts, on_device(): return work.reshape(kernel.shape)  44.5 us
    dot_general x3, matrix products, update(): jnp.einsum('rib,cjb->ricj', factors[1], factors[2][start:stop], precision...  43 us
    another operation x5, other arithmetic, factor(): inverse = jax.scipy.linalg.solve_triangular(lower, eye, lower=True)  42 us
  transfers between devices with their start and end apart: 6, of which 6 were waited for; matrix products, arithmetic and copies ran while one was open for 4% of the time, Pallas kernels for 0%

commit v1 on v0

v1 whole, which is shorter than its diff:
```python
import functools

import jax
import jax.numpy as jnp
from jax import lax
from jax.experimental import pallas as pl
from jax.experimental.pallas import tpu as pltpu
from jax.sharding import PartitionSpec as P

STEPS = 2
TILE = 128
SUB = 8
HIGH = lax.Precision.HIGHEST


def dot_nn(a, b):
    return lax.dot_general(
        a, b, (((1,), (0,)), ((), ())), precision=HIGH, preferred_element_type=jnp.float32
    )


def dot_nt(a, b):
    return lax.dot_general(
        a, b, (((1,), (1,)), ((), ())), precision=HIGH, preferred_element_type=jnp.float32
    )


def split(x):
    hi = x.astype(jnp.bfloat16)
    lo = (x - hi.astype(jnp.float32)).astype(jnp.bfloat16)
    return hi, lo


def factor_tile(tile):
    count = TILE // SUB
    row = lax.broadcasted_iota(jnp.int32, (SUB, TILE), 0)
    lane = lax.broadcasted_iota(jnp.int32, (SUB, TILE), 1)
    upper = [tile[SUB * r : SUB * (r + 1), :] for r in range(count)]
    inverse = [jnp.where(lane == row + SUB * r, 1.0, 0.0) for r in range(count)]
    for g in range(count):
        cols = [
            [
                jnp.broadcast_to(upper[r][:, SUB * g + j : SUB * g + j + 1], (SUB, TILE))
                for r in range(g, count)
            ]
            for j in range(SUB)
        ]
        scale = jnp.zeros((SUB, TILE), jnp.float32)
        for j in range(SUB):
            pivot = jnp.broadcast_to(cols[j][0][j : j + 1, :], (SUB, TILE))
            scale = jnp.where(row == j, pivot, scale)
            recip = 1.0 / pivot
            row_u = jnp.broadcast_to(upper[g][j : j + 1, :], (SUB, TILE)) * recip
            row_i = jnp.broadcast_to(inverse[g][j : j + 1, :], (SUB, TILE)) * recip
            heads = [
                jnp.broadcast_to(cols[j2][0][j : j + 1, :], (SUB, TILE)) * recip
                for j2 in range(j + 1, SUB)
            ]
            for r in range(g, count):
                f = cols[j][r - g]
                if r == g:
                    f = jnp.where(row > j, f, 0.0)
                upper[r] = upper[r] - f * row_u
                inverse[r] = inverse[r] - f * row_i
                for j2 in range(j + 1, SUB):
                    cols[j2][r - g] = cols[j2][r - g] - f * heads[j2 - j - 1]
        root = lax.rsqrt(scale)
        upper[g] = jnp.where(lane >= row + SUB * g, upper[g] * root, 0.0)
        inverse[g] = jnp.where(lane <= row + SUB * g, inverse[g] * root, 0.0)
    return jnp.concatenate(upper, axis=0), jnp.concatenate(inverse, axis=0)


def factor_kernel(d_ref, l_ref, w_ref, work):
    n = d_ref.shape[0]
    work[...] = d_ref[...]
    l_ref[...] = jnp.zeros_like(l_ref)
    w_ref[...] = jnp.where(
        lax.broadcasted_iota(jnp.int32, (n, n), 0) == lax.broadcasted_iota(jnp.int32, (n, n), 1),
        1.0,
        0.0,
    )
    rows = lax.broadcasted_iota(jnp.int32, (n, TILE), 0)

    def step(t, carry):
        at = pl.ds(pl.multiple_of(t * TILE, TILE), TILE)
        upper, inverse = factor_tile(work[at, at])
        panel = dot_nt(work[:, at], inverse)
        below = jnp.where(rows >= (t + 1) * TILE, panel, 0.0)
        l_ref[:, at] = below
        l_ref[at, at] = upper.T
        work[...] = work[...] - dot_nt(below, below)
        head = dot_nn(inverse, w_ref[at, :])
        w_ref[...] = w_ref[...] - dot_nn(below, head)
        w_ref[at, :] = head
        return carry

    lax.fori_loop(0, n // TILE, step, 0)


def factor(diag):
    n = diag.shape[0]
    out = jax.ShapeDtypeStruct((n, n), jnp.float32)
    return pl.pallas_call(
        factor_kernel,
        out_shape=(out, out),
        in_specs=[pl.BlockSpec(memory_space=pltpu.VMEM)],
        out_specs=(pl.BlockSpec(memory_space=pltpu.VMEM),) * 2,
        scratch_shapes=[pltpu.VMEM((n, n), jnp.float32)],
        compiler_params=pltpu.CompilerParams(vmem_limit_bytes=32 * 2**20),
        cost_estimate=pl.CostEstimate(flops=2 * n**3, bytes_accessed=12 * n * n, transcendentals=0),
    )(diag)


def update_kernel(rows, blk, lbc, m_ref, r_ref, c_ref, w_ref, l_ref, out_ref, cols):
    a = pl.program_id(0)
    row_id = a * rows + lax.axis_index("prow")
    q = lax.axis_index("pcol")
    lanes = blk // TILE
    pitch = lbc * lanes
    depth = STEPS * blk

    @pl.when(a == 0)
    def _():
        def prepare(b, carry):
            raw = jnp.concatenate([c_ref[k, b] for k in range(STEPS)], axis=0)
            hi, lo = split(dot_nn(w_ref[...], raw))
            cols[b, 0:depth, :] = hi
            cols[b, depth : 2 * depth, :] = hi
            cols[b, 2 * depth : 3 * depth, :] = lo
            return carry

        lax.fori_loop(0, lbc, prepare, 0)

    def store(b, value):
        for h in range(lanes):
            at = pl.ds(lanes * b + h, blk, stride=pitch)
            out_ref[at, :] = value[:, h * TILE : (h + 1) * TILE]

    @pl.when(row_id < STEPS)
    def _():
        out_ref[...] = jnp.zeros_like(out_ref)
        for i in range(STEPS):
            for j in range(i + 1):

                @pl.when((row_id == i) & (q == j))
                def _():
                    store(0, l_ref[i * blk : (i + 1) * blk, j * blk : (j + 1) * blk])

    @pl.when(row_id >= STEPS)
    def _():
        raw = jnp.concatenate([r_ref[k, 0] for k in range(STEPS)], axis=1)
        panel = dot_nt(raw, w_ref[...])
        hi, lo = split(panel)
        left = jnp.concatenate([hi, lo, hi], axis=1)
        for b in range(lbc):
            delta = jnp.dot(left, cols[b], preferred_element_type=jnp.float32)
            for h in range(lanes):
                at = pl.ds(lanes * b + h, blk, stride=pitch)
                out_ref[at, :] = m_ref[at, :] - delta[:, h * TILE : (h + 1) * TILE]
        for j in range(STEPS):

            @pl.when(q == j)
            def _():
                store(0, panel[:, j * blk : (j + 1) * blk])


def update(flat, row_panel, col_panel, inverse, lower, rows):
    _, lbr, blk, _ = row_panel.shape
    lbc = col_panel.shape[1]
    depth = STEPS * blk
    stripe = blk * lbc * (blk // TILE)
    whole = pl.BlockSpec((depth, depth), lambda a: (0, 0))
    return pl.pallas_call(
        functools.partial(update_kernel, rows, blk, lbc),
        grid=(lbr,),
        out_shape=jax.ShapeDtypeStruct(flat.shape, jnp.float32),
        in_specs=[
            pl.BlockSpec((stripe, TILE), lambda a: (a, 0)),
            pl.BlockSpec((STEPS, 1, blk, blk), lambda a: (0, a, 0, 0)),
            pl.BlockSpec((STEPS, lbc, blk, blk), lambda a: (0, 0, 0, 0)),
            whole,
            whole,
        ],
        out_specs=pl.BlockSpec((stripe, TILE), lambda a: (a, 0)),
        scratch_shapes=[pltpu.VMEM((lbc, 3 * depth, blk), jnp.bfloat16)],
        compiler_params=pltpu.CompilerParams(vmem_limit_bytes=56 * 2**20),
        cost_estimate=pl.CostEstimate(
            flops=6 * flat.size * depth, bytes_accessed=8 * flat.size, transcendentals=0
        ),
    )(flat, row_panel, col_panel, inverse, lower)


def on_device(kernel):
    rows = lax.axis_size("prow")
    p = lax.axis_index("prow")
    q = lax.axis_index("pcol")
    lbr, blk, lbc = (kernel.shape[0], kernel.shape[2], kernel.shape[3])
    flat = kernel.reshape(lbr * blk * lbc * (blk // TILE), TILE)
    column = kernel[:, 0, :, 0, 0, :]
    across = kernel[0, 0, :, :, 0, :].transpose(1, 0, 2)

    blocks = [
        jnp.where((p == i) & (q == j), column[0], 0.0) for i in range(STEPS) for j in range(i + 1)
    ]
    d00, d10, d11 = lax.psum(jnp.stack(blocks), ("prow", "pcol"))
    diag = jnp.block([[d00, d10.T], [d10, d11]])
    row_panel = lax.psum(
        jnp.stack([jnp.where(q == k, column, 0.0) for k in range(STEPS)]), "pcol"
    )
    col_panel = lax.psum(
        jnp.stack([jnp.where(p == k, across, 0.0) for k in range(STEPS)]), "prow"
    )
    lower, inverse = factor(diag)
    out = update(flat, row_panel, col_panel, inverse, lower, rows)
    return out.reshape(kernel.shape)


def solution(mesh):
    in_specs = (P(None, "prow", None, None, "pcol", None),)
    out_specs = P(None, "prow", None, None, "pcol", None)
    return jax.shard_map(
        on_device, mesh=mesh, in_specs=in_specs, out_specs=out_specs, check_vma=False
    )
```

time: 700 us -> 422 us (0.60); the launches traced: 686 us -> 420 us
  other arithmetic: 138 us -> 7.69 us
  local copies, waits for them, and re-layouts: 114 us -> 7.1 us
  Pallas kernels: 0 us -> 71.6 us
  matrix products: 58 us -> 0 us
  waiting for transfers between devices: 358 us -> 321 us
    another operation x18 -> x4, other arithmetic: 112 us -> 7.2 us  [the longest x2 4.23 us: on_device(): jnp.stack([jnp.where(p == k, across, 0.0) for k in range(STEPS)])]
    pallas_call x0 -> x2, Pallas kernels: none -> 71.6 us  [the longest x1 43.9 us: update(): pl.pallas_call(functools.partial(update_kernel, rows, blk, lbc), grid=(lb...]
    dot_general x5 -> x0, matrix products: 51.9 us -> none  [the longest x3 43 us: update(): jnp.einsum('rib,cjb->ricj', factors[1], factors[2][start:stop], precision...]
    reshape x1 -> x0, local copies, waits for them, and re-layouts: 44.5 us -> none  [on_device(): return work.reshape(kernel.shape)]
    unnamed x23 -> x5, local copies, waits for them, and re-layouts: 45.9 us -> 2.15 us
    psum x6 -> x3, waiting for transfers between devices: 358 us -> 321 us  [the longest x1 138 us: on_device(): lax.psum(jnp.stack([jnp.where(p == k, across, 0.0) for k in range(STEPS)]...]
    select_n x9 -> x2, other arithmetic: 14.4 us -> 0.36 us  [the longest x1 0.29 us: on_device(): jnp.where(q == k, column, 0.0)]
    another operation x19 -> x1, local copies, waits for them, and re-layouts: 11.7 us -> 1.19 us  [on_device(): d00, d10, d11 = lax.psum(jnp.stack(blocks), ('prow', 'pcol'))]
  transfers between devices with their start and end apart: 6 -> 3, of which waited for: 6 -> 3; matrix products, arithmetic and copies ran while one was open for 4% -> 2% of each run, Pallas kernels for 0% -> 7%
where the time goes in v1:
time: 422 us; the launch traced here: 420 us
  waiting for transfers between devices  321 us (76%)
  Pallas kernels  71.6 us (17%)
  between operations  13.2 us (3%)
  other arithmetic  7.69 us (2%)
  local copies, waits for them, and re-layouts  7.1 us (2%)
    psum x1, waiting for transfers between devices, on_device(): lax.psum(jnp.stack([jnp.where(p == k, across, 0.0) for k in range(STEPS)]...  138 us
    psum x1, waiting for transfers between devices, on_device(): d00, d10, d11 = lax.psum(jnp.stack(blocks), ('prow', 'pcol'))  122 us
    psum x1, waiting for transfers between devices, on_device(): lax.psum(jnp.stack([jnp.where(q == k, column, 0.0) for k in range(STEPS)]...  60.7 us
    pallas_call x1, Pallas kernels, update(): pl.pallas_call(functools.partial(update_kernel, rows, blk, lbc), grid=(lb...  43.9 us
    pallas_call x1, Pallas kernels, factor(): pl.pallas_call(factor_kernel, out_shape=(out, out), in_specs=[pl.BlockSpe...  27.7 us
  transfers between devices with their start and end apart: 3, of which 3 were waited for; matrix products, arithmetic and copies ran while one was open for 2% of the time, Pallas kernels for 7%

profile of v1, /device:TPU:29, one launch (start us, length us, event | category | flops | bytes accessed | tf_op | source)
XLA Modules:
  0.0 420.3 jit_solution(13718124690928253397)
XLA Ops:
  6.5 0.0 all-reduce.8.cloned.1.call-start
  6.5 1.1 slice.15
  7.7 0.0 slice-start
  7.7 0.1 select_bitcast_fusion.6
  7.8 0.9 pad_maximum_fusion.2
  8.7 0.0 all-reduce.8.cloned.1.call-update
  8.7 0.0 all-reduce.4.cloned.1.call-start
  8.8 0.6 slice-done
  9.4 0.3 select_bitcast_fusion.3
  9.7 2.0 pad_maximum_fusion.1
  11.7 0.0 all-reduce.4.cloned.1.call-update
  11.7 0.0 slice-start.1
  11.7 0.0 all-reduce.6.cloned.1.call-start
  11.8 1.8 slice-done.1
  13.6 0.9 select_bitcast_fusion.1
  14.5 3.4 pad_maximum_fusion
  17.9 0.0 all-reduce.6.cloned.1.call-update
  17.9 121.9 %all-reduce.8.cloned.1.call-done = f32[3,256,256]{2,1,0:T(8,128)} async-done(((f32[3,256,256]{2,1,0:T(8,128)}), f32[3,256,256]{2,1,0:T(8,128)}) %all-reduce.8.cloned.1.call-update) | async-done | bytes 786448 | tf_op jit(solution)/shard_map/psum | solution.py:205
  139.8 1.2 fusion
  141.0 0.1 copy.17
  141.2 0.2 copy.12
  141.4 0.1 maximum_maximum_fusion.d_ref
  141.5 27.7 %shard_map.17 = (f32[512,512]{1,0:T(8,128)S(1)}, f32[512,512]{1,0:T(8,128)S(1)}) custom-call(f32[512,512]{1,0:T(8,128)S(1)} %maximum_maximum_fusion.d_ref), custom_call_target="tpu_custom_call" | custom-call | flops 268435456 | bytes 3145728 | tf_op jit(solution)/shard_map/pallas_call | solution.py:103
  169.2 0.0 copy-start
  169.2 1.0 copy-done
  170.2 0.0 copy-start.1
  170.2 1.0 copy-done.1
  171.2 60.7 %all-reduce.4.cloned.1.call-done.r_ref = f32[2,6,256,256]{3,2,1,0:T(8,128)} async-done(((f32[2,6,256,256]{3,2,1,0:T(8,128)}), f32[2,6,256,256]{3,2,1,0:T(8,128)}) %all-reduce.4.cloned.1.call-update) | async-done | bytes 3145744 | tf_op jit(solution)/shard_map/psum | solution.py:207
  232.0 137.9 %all-reduce.6.cloned.1.call-done.c_ref = f32[2,12,256,256]{3,2,1,0:T(8,128)} async-done(((f32[2,12,256,256]{3,2,1,0:T(8,128)}), f32[2,12,256,256]{3,2,1,0:T(8,128)}) %all-reduce.6.cloned.1.call-update) | async-done | bytes 6291472 | tf_op jit(solution)/shard_map/psum | solution.py:210
  369.9 43.9 %shard_map.18 = f32[36864,128]{1,0:T(8,128)} custom-call(f32[36864,128]{1,0:T(8,128)} %bitcast.32, f32[2,6,256,256]{3,2,1,0:T(8,128)} %all-reduce.4.cloned.1.call-done.r_ref, f32[2,12,256,256]{3,2,1,0:T(8,128)} %all-reduce.6.cloned.1.call-done.c_ref, f32[512,512]{1,0:T(8,128)} %copy-done.1, f32[512,512]{1,0:T(8,128)} %copy-done), custom_call_target="tpu_custom_call" | custom-call | flops 14495514624 | bytes 37748736 | tf_op jit(solution)/shard_map/pallas_call | solution.py:173
  (1 shorter events, 0.0 us)
Async XLA Ops:
  6.5 133.2 %all-reduce.8.cloned.1.call-start = ((), (), s32[]{:S(2)}) async-start(), calls=%async_computation.2 | async-start | bytes 1572864 | tf_op jit(solution)/shard_map/psum | solution.py:205
  7.7 1.7 slice-start
  8.7 223.2 %all-reduce.4.cloned.1.call-start = ((), (), s32[]{:S(2)}) async-start(), calls=%async_computation | async-start | bytes 6291456 | tf_op jit(solution)/shard_map/psum | solution.py:207
  11.7 1.9 slice-start.1
  11.7 358.1 %all-reduce.6.cloned.1.call-start = ((), (), s32[]{:S(2)}) async-start(), calls=%async_computation.1 | async-start | bytes 12582912 | tf_op jit(solution)/shard_map/psum | solution.py:210
  169.2 1.0 copy-start
  170.2 1.1 copy-start.1
Sparse Core Ops, SparseCore 0:
  12.5 127.1 all-reduce.7
  143.2 88.7 all-reduce.3
  234.3 135.4 all-reduce.5

commit v2 on v1

--- a/solution.py
+++ b/solution.py
@@ -165,10 +165,11 @@
 
 
 def update(flat, row_panel, col_panel, inverse, lower, rows):
-    _, lbr, blk, _ = row_panel.shape
+    blk = row_panel.shape[2]
     lbc = col_panel.shape[1]
     depth = STEPS * blk
     stripe = blk * lbc * (blk // TILE)
+    lbr = flat.shape[0] // stripe
     whole = pl.BlockSpec((depth, depth), lambda a: (0, 0))
     return pl.pallas_call(
         functools.partial(update_kernel, rows, blk, lbc),
@@ -190,26 +191,167 @@
     )(flat, row_panel, col_panel, inverse, lower)
 
 
+def copy_kernel(rows, cols, column, across, r_out, c_out, r_recv, c_recv, r_send, z_send, pair_send):
+    lbr, lbc = column.shape[0], across.shape[0]
+    bits = cols.bit_length() - 1
+    p = lax.axis_index("prow")
+    q = lax.axis_index("pcol")
+    own = p % 2
+    other = 1 - own
+    pair = p + 1 - 2 * own
+    has_next = p + 2 < rows
+
+    def flipped(value, bit):
+        return value + 2**bit * (1 - 2 * ((value // 2**bit) % 2))
+
+    barrier = pltpu.get_barrier_semaphore()
+
+    def greet(to_p, to_q):
+        pl.semaphore_signal(
+            barrier, inc=1, device_id=(to_p, to_q), device_id_type=pl.DeviceIdType.MESH
+        )
+
+    greet(pair, q)
+    for bit in range(bits):
+        greet(p, flipped(q, bit))
+
+    @pl.when(has_next)
+    def _():
+        greet(p + 2, q)
+
+    @pl.when(p >= 2)
+    def _():
+        greet(p - 2, q)
+
+    chain = jnp.where(has_next, 1, 0) + jnp.where(p >= 2, 1, 0)
+    pl.semaphore_wait(barrier, 1 + bits + chain)
+
+    def remote(ref, send, recv, to_p, to_q):
+        return pltpu.make_async_remote_copy(
+            src_ref=ref,
+            dst_ref=ref,
+            send_sem=send,
+            recv_sem=recv,
+            device_id=(to_p, to_q),
+            device_id_type=pl.DeviceIdType.MESH,
+        )
+
+    def c_local(b):
+        return pltpu.make_async_copy(across.at[b], c_out.at[own, b], c_recv.at[own, b])
+
+    def c_next(b):
+        return remote(c_out.at[own, b], z_send.at[b], c_recv.at[own, b], p + 2, q)
+
+    def c_pair(b):
+        return remote(c_out.at[own, b], pair_send.at[b], c_recv.at[own, b], pair, q)
+
+    def c_arrived(k, b):
+        pltpu.make_async_copy(across.at[b], c_out.at[k, b], c_recv.at[k, b]).wait()
+
+    order = [q, flipped(q, 0)]
+
+    def r_local(k, a):
+        source = column.at[a] if a < lbr else c_out.at[a - lbr, 0]
+        return pltpu.make_async_copy(source, r_out.at[k, a], r_recv.at[k, a])
+
+    def r_child(k, a, bit):
+        to_q = flipped(q, bit)
+        return remote(r_out.at[k, a], r_send.at[k, a, bit], r_recv.at[k, a], p, to_q)
+
+    def sends(k, bit):
+        return order[k] % 2 ** (bit + 1) == 0
+
+    for k in range(STEPS):
+
+        @pl.when(order[k] == 0)
+        def _():
+            for a in range(lbr):
+                r_local(k, a).start()
+
+    @pl.when(p < 2)
+    def _():
+        for b in range(lbc):
+            c_local(b).start()
+
+    for s in range(max(lbc, lbr + STEPS)):
+        if s < lbc:
+            c_arrived(own, s)
+
+            @pl.when(has_next)
+            def _():
+                c_next(s).start()
+
+            c_pair(s).start()
+        if s == lbr:
+            c_arrived(other, 0)
+            for k in range(STEPS):
+
+                @pl.when(order[k] == 0)
+                def _():
+                    for a in range(lbr, lbr + STEPS):
+                        r_local(k, a).start()
+
+        if s < lbr + STEPS:
+            for k in range(STEPS):
+                r_local(k, s).wait()
+                for bit in reversed(range(bits)):
+
+                    @pl.when(sends(k, bit))
+                    def _():
+                        r_child(k, s, bit).start()
+
+    for b in range(1, lbc):
+        c_arrived(other, b)
+    for b in range(lbc):
+        c_pair(b).wait_send()
+
+        @pl.when(has_next)
+        def _():
+            c_next(b).wait_send()
+
+    for k in range(STEPS):
+        for bit in range(bits):
+
+            @pl.when(sends(k, bit))
+            def _():
+                for a in range(lbr + STEPS):
+                    r_child(k, a, bit).wait_send()
+
+
+def exchange(column, across, rows, cols):
+    lbr, blk, _ = column.shape
+    lbc = across.shape[0]
+    bits = cols.bit_length() - 1
+    anywhere = pl.BlockSpec(memory_space=pl.ANY)
+    return pl.pallas_call(
+        functools.partial(copy_kernel, rows, cols),
+        out_shape=(
+            jax.ShapeDtypeStruct((STEPS, lbr + STEPS, blk, blk), jnp.float32),
+            jax.ShapeDtypeStruct((STEPS, lbc, blk, blk), jnp.float32),
+        ),
+        in_specs=[anywhere, anywhere],
+        out_specs=(anywhere, anywhere),
+        scratch_shapes=[
+            pltpu.SemaphoreType.DMA((STEPS, lbr + STEPS)),
+            pltpu.SemaphoreType.DMA((STEPS, lbc)),
+            pltpu.SemaphoreType.DMA((STEPS, lbr + STEPS, bits)),
+            pltpu.SemaphoreType.DMA((lbc,)),
+            pltpu.SemaphoreType.DMA((lbc,)),
+        ],
+        compiler_params=pltpu.CompilerParams(collective_id=0, has_side_effects=True),
+    )(column, across)
+
+
 def on_device(kernel):
     rows = lax.axis_size("prow")
-    p = lax.axis_index("prow")
-    q = lax.axis_index("pcol")
     lbr, blk, lbc = (kernel.shape[0], kernel.shape[2], kernel.shape[3])
     flat = kernel.reshape(lbr * blk * lbc * (blk // TILE), TILE)
     column = kernel[:, 0, :, 0, 0, :]
     across = kernel[0, 0, :, :, 0, :].transpose(1, 0, 2)
 
-    blocks = [
-        jnp.where((p == i) & (q == j), column[0], 0.0) for i in range(STEPS) for j in range(i + 1)
-    ]
-    d00, d10, d11 = lax.psum(jnp.stack(blocks), ("prow", "pcol"))
-    diag = jnp.block([[d00, d10.T], [d10, d11]])
-    row_panel = lax.psum(
-        jnp.stack([jnp.where(q == k, column, 0.0) for k in range(STEPS)]), "pcol"
-    )
-    col_panel = lax.psum(
-        jnp.stack([jnp.where(p == k, across, 0.0) for k in range(STEPS)]), "prow"
-    )
+    row_panel, col_panel = exchange(column, across, rows, lax.axis_size("pcol"))
+    d00, d10 = row_panel[0, lbr], row_panel[0, lbr + 1]
+    diag = jnp.block([[d00, jnp.zeros_like(d00)], [d10, row_panel[1, lbr + 1]]])
     lower, inverse = factor(diag)
     out = update(flat, row_panel, col_panel, inverse, lower, rows)
     return out.reshape(kernel.shape)

time: 422 us -> 307 us (0.73)
  waiting for transfers between devices: 321 us -> 0 us
  Pallas kernels: 71.6 us -> 293 us
  between operations: 13.2 us -> 0.05 us
  other arithmetic: 7.69 us -> 0.12 us
  local copies, waits for them, and re-layouts: 7.1 us -> 13.2 us
    psum x3 -> x0, waiting for transfers between devices: 321 us -> none  [the longest x1 138 us: on_device(): lax.psum(jnp.stack([jnp.where(p == k, across, 0.0) for k in range(STEPS)]...]
    pallas_call x0 -> x1, Pallas kernels: none -> 222 us  [exchange(): pl.pallas_call(functools.partial(copy_kernel, rows, cols), out_shape=(jax...]
    another operation x4 -> x0, other arithmetic: 7.2 us -> none  [the longest x2 4.23 us: on_device(): jnp.stack([jnp.where(p == k, across, 0.0) for k in range(STEPS)])]
  transfers between devices with their start and end apart: 3 -> 0, of which waited for: 3 -> 0; matrix products, arithmetic and copies ran while one was open for 2% -> 0% of each run, Pallas kernels for 7% -> 0%
where the time goes in v2:
time: 307 us
  Pallas kernels  293 us (95%)
  local copies, waits for them, and re-layouts  13.2 us (4%)
    pallas_call x1, Pallas kernels, exchange(): pl.pallas_call(functools.partial(copy_kernel, rows, cols), out_shape=(jax...  222 us
    pallas_call x1, Pallas kernels, update(): pl.pallas_call(functools.partial(update_kernel, rows, blk, lbc), grid=(lb...  43.9 us
    pallas_call x1, Pallas kernels, factor(): pl.pallas_call(factor_kernel, out_shape=(out, out), in_specs=[pl.BlockSpe...  27.5 us

profile of v2, /device:TPU:29, one launch (start us, length us, event | category | flops | bytes accessed | tf_op | source)
XLA Modules:
  0.0 306.5 jit_solution(2390496243527732751)
XLA Ops:
  0.0 2.5 slice.15
  2.5 1.3 copy.13
  3.8 4.0 %slice.16 = f32[1,1,256,12,1,256]{5,4,3,2,1,0:T(1,128)S(1)} slice(f32[6,1,256,12,1,256]{5,4,3,2,1,0:T(1,128)} %param.1), slice={[0:1], [0:1], [0:256], [0:12], [0:1], [0:256]} | slice | bytes 6291456 | tf_op jit(solution)/shard_map/slice | solution.py:350
  7.9 2.2 copy.12
  10.1 221.7 %shard_map.17 = (f32[2,8,256,256]{3,2,1,0:T(8,128)}, f32[2,12,256,256]{3,2,1,0:T(8,128)}) custom-call(f32[6,256,256]{2,1,0:T(8,128)} %bitcast.17, f32[12,256,256]{2,1,0:T(8,128)} %bitcast.16), custom_call_target="tpu_custom_call" | custom-call | tf_op jit(solution)/shard_map/pallas_call | solution.py:326
  231.8 1.2 slice_bitcast_fusion.1
  233.0 0.1 select_maximum_fusion.d_ref
  233.1 27.5 %shard_map.18 = (f32[512,512]{1,0:T(8,128)S(1)}, f32[512,512]{1,0:T(8,128)S(1)}) custom-call(f32[512,512]{1,0:T(8,128)S(1)} %select_maximum_fusion.d_ref), custom_call_target="tpu_custom_call" | custom-call | flops 268435456 | bytes 3145728 | tf_op jit(solution)/shard_map/pallas_call | solution.py:103
  260.7 0.0 copy-start
  260.7 1.0 copy-done
  261.6 0.0 copy-start.1
  261.6 1.0 copy-done.1
  262.6 43.9 %shard_map.19 = f32[36864,128]{1,0:T(8,128)} custom-call(f32[36864,128]{1,0:T(8,128)} %bitcast.18, f32[2,8,256,256]{3,2,1,0:T(8,128)} %get-tuple-element.9.r_ref, f32[2,12,256,256]{3,2,1,0:T(8,128)} %get-tuple-element.10.c_ref, f32[512,512]{1,0:T(8,128)} %copy-done.1, f32[512,512]{1,0:T(8,128)} %copy-done), custom_call_target="tpu_custom_call" | custom-call | flops 14495514624 | bytes 37748736 | tf_op jit(solution)/shard_map/pallas_call | solution.py:174
Async XLA Ops:
  260.7 1.0 copy-start
  261.6 1.0 copy-start.1

commit v3 on v2

--- a/solution.py
+++ b/solution.py
@@ -123,10 +123,12 @@
     def _():
         def prepare(b, carry):
             raw = jnp.concatenate([c_ref[k, b] for k in range(STEPS)], axis=0)
-            hi, lo = split(dot_nn(w_ref[...], raw))
-            cols[b, 0:depth, :] = hi
-            cols[b, depth : 2 * depth, :] = hi
-            cols[b, 2 * depth : 3 * depth, :] = lo
+            for k in range(STEPS):
+                at, used = k * blk, (k + 1) * blk
+                hi, lo = split(dot_nn(w_ref[at:used, :used], raw[:used]))
+                cols[b, at:used, :] = hi
+                cols[b, depth + at : depth + used, :] = hi
+                cols[b, 2 * depth + at : 2 * depth + used, :] = lo
             return carry
 
         lax.fori_loop(0, lbc, prepare, 0)
@@ -149,7 +151,11 @@
     @pl.when(row_id >= STEPS)
     def _():
         raw = jnp.concatenate([r_ref[k, 0] for k in range(STEPS)], axis=1)
-        panel = dot_nt(raw, w_ref[...])
+        parts = []
+        for k in range(STEPS):
+            at, used = k * blk, (k + 1) * blk
+            parts.append(dot_nt(raw[:, :used], w_ref[at:used, :used]))
+        panel = jnp.concatenate(parts, axis=1)
         hi, lo = split(panel)
         left = jnp.concatenate([hi, lo, hi], axis=1)
         for b in range(lbc):
@@ -293,12 +299,23 @@
 
         if s < lbr + STEPS:
             for k in range(STEPS):
-                r_local(k, s).wait()
+
+                @pl.when(order[k] % 2 == 0)
+                def _():
+                    r_local(k, s).wait()
+
                 for bit in reversed(range(bits)):
 
                     @pl.when(sends(k, bit))
                     def _():
                         r_child(k, s, bit).start()
+
+    for k in range(STEPS):
+
+        @pl.when(order[k] % 2 == 1)
+        def _():
+            for a in range(lbr + STEPS):
+                r_local(k, a).wait()
 
     for b in range(1, lbc):
         c_arrived(other, b)

time: 307 us -> 292 us (0.951)
  Pallas kernels: 293 us -> 279 us
    pallas_call x1, Pallas kernels: 222 us -> 208 us  [exchange(): pl.pallas_call(functools.partial(copy_kernel, rows, cols), out_shape=(jax...]
where the time goes in v3:
time: 292 us
  Pallas kernels  279 us (96%)
  local copies, waits for them, and re-layouts  13.2 us (5%)
    pallas_call x1, Pallas kernels, exchange(): pl.pallas_call(functools.partial(copy_kernel, rows, cols), out_shape=(jax...  208 us
    pallas_call x1, Pallas kernels, update(): pl.pallas_call(functools.partial(update_kernel, rows, blk, lbc), grid=(lb...  43.6 us
    pallas_call x1, Pallas kernels, factor(): pl.pallas_call(factor_kernel, out_shape=(out, out), in_specs=[pl.BlockSpe...  27.5 us

profile of v3, /device:TPU:29, one launch (start us, length us, event | category | flops | bytes accessed | tf_op | source)
XLA Modules:
  0.0 292.2 jit_solution(13632261636060144582)
XLA Ops:
  0.0 2.5 slice.15
  2.5 1.3 copy.13
  3.8 4.0 %slice.16 = f32[1,1,256,12,1,256]{5,4,3,2,1,0:T(1,128)S(1)} slice(f32[6,1,256,12,1,256]{5,4,3,2,1,0:T(1,128)} %param.1), slice={[0:1], [0:1], [0:256], [0:12], [0:1], [0:256]} | slice | bytes 6291456 | tf_op jit(solution)/shard_map/slice | solution.py:367
  7.9 2.2 copy.12
  10.1 207.6 %shard_map.17 = (f32[2,8,256,256]{3,2,1,0:T(8,128)}, f32[2,12,256,256]{3,2,1,0:T(8,128)}) custom-call(f32[6,256,256]{2,1,0:T(8,128)} %bitcast.17, f32[12,256,256]{2,1,0:T(8,128)} %bitcast.16), custom_call_target="tpu_custom_call" | custom-call | tf_op jit(solution)/shard_map/pallas_call | solution.py:343
  217.7 1.2 slice_bitcast_fusion.1
  218.9 0.1 select_maximum_fusion.d_ref
  219.0 27.5 %shard_map.18 = (f32[512,512]{1,0:T(8,128)S(1)}, f32[512,512]{1,0:T(8,128)S(1)}) custom-call(f32[512,512]{1,0:T(8,128)S(1)} %select_maximum_fusion.d_ref), custom_call_target="tpu_custom_call" | custom-call | flops 268435456 | bytes 3145728 | tf_op jit(solution)/shard_map/pallas_call | solution.py:103
  246.6 0.0 copy-start
  246.6 1.0 copy-done
  247.6 0.0 copy-start.1
  247.6 1.0 copy-done.1
  248.5 43.6 %shard_map.19 = f32[36864,128]{1,0:T(8,128)} custom-call(f32[36864,128]{1,0:T(8,128)} %bitcast.18, f32[2,8,256,256]{3,2,1,0:T(8,128)} %get-tuple-element.9.r_ref, f32[2,12,256,256]{3,2,1,0:T(8,128)} %get-tuple-element.10.c_ref, f32[512,512]{1,0:T(8,128)} %copy-done.1, f32[512,512]{1,0:T(8,128)} %copy-done), custom_call_target="tpu_custom_call" | custom-call | flops 14495514624 | bytes 37748736 | tf_op jit(solution)/shard_map/pallas_call | solution.py:180
Async XLA Ops:
  246.6 1.0 copy-start
  247.6 1.0 copy-start.1

commit v4 on v3

--- a/solution.py
+++ b/solution.py
@@ -339,15 +339,15 @@
     lbr, blk, _ = column.shape
     lbc = across.shape[0]
     bits = cols.bit_length() - 1
-    anywhere = pl.BlockSpec(memory_space=pl.ANY)
+    held = pl.BlockSpec(memory_space=pltpu.VMEM)
     return pl.pallas_call(
         functools.partial(copy_kernel, rows, cols),
         out_shape=(
             jax.ShapeDtypeStruct((STEPS, lbr + STEPS, blk, blk), jnp.float32),
             jax.ShapeDtypeStruct((STEPS, lbc, blk, blk), jnp.float32),
         ),
-        in_specs=[anywhere, anywhere],
-        out_specs=(anywhere, anywhere),
+        in_specs=[held, held],
+        out_specs=(held, held),
         scratch_shapes=[
             pltpu.SemaphoreType.DMA((STEPS, lbr + STEPS)),
             pltpu.SemaphoreType.DMA((STEPS, lbc)),
@@ -355,7 +355,9 @@
             pltpu.SemaphoreType.DMA((lbc,)),
             pltpu.SemaphoreType.DMA((lbc,)),
         ],
-        compiler_params=pltpu.CompilerParams(collective_id=0, has_side_effects=True),
+        compiler_params=pltpu.CompilerParams(
+            collective_id=0, has_side_effects=True, vmem_limit_bytes=40 * 2**20
+        ),
     )(column, across)
 
 

time: 292 us -> 169 us (0.58)
  Pallas kernels: 279 us -> 160 us
  local copies, waits for them, and re-layouts: 13.2 us -> 9.34 us
    pallas_call x1, Pallas kernels: 208 us -> 88.4 us  [exchange(): pl.pallas_call(functools.partial(copy_kernel, rows, cols), out_shape=(jax...]
where the time goes in v4:
time: 169 us
  Pallas kernels  160 us (95%)
  local copies, waits for them, and re-layouts  9.34 us (6%)
    pallas_call x1, Pallas kernels, exchange(): pl.pallas_call(functools.partial(copy_kernel, rows, cols), out_shape=(jax...  88.4 us
    pallas_call x1, Pallas kernels, update(): pl.pallas_call(functools.partial(update_kernel, rows, blk, lbc), grid=(lb...  43.6 us
    pallas_call x1, Pallas kernels, factor(): pl.pallas_call(factor_kernel, out_shape=(out, out), in_specs=[pl.BlockSpe...  27.5 us
    slice x1, local copies, waits for them, and re-layouts, on_device(): across = kernel[0, 0, :, :, 0, :].transpose(1, 0, 2)  4.05 us

profile of v4, /device:TPU:29, one launch (start us, length us, event | category | flops | bytes accessed | tf_op | source)
XLA Modules:
  0.0 169.1 jit_solution(2230965191607838945)
XLA Ops:
  0.0 2.5 %slice.15 = f32[6,1,256,1,1,256]{5,4,3,2,1,0:T(1,128)S(1)} slice(f32[6,1,256,12,1,256]{5,4,3,2,1,0:T(1,128)} %param.1), slice={[0:6], [0:1], [0:256], [0:1], [0:1], [0:256]} | slice | bytes 3145728 | tf_op jit(solution)/shard_map/slice | solution.py:368
  2.5 0.2 copy.13
  2.7 4.0 %slice.16 = f32[1,1,256,12,1,256]{5,4,3,2,1,0:T(1,128)S(1)} slice(f32[6,1,256,12,1,256]{5,4,3,2,1,0:T(1,128)} %param.1), slice={[0:1], [0:1], [0:256], [0:12], [0:1], [0:256]} | slice | bytes 6291456 | tf_op jit(solution)/shard_map/slice | solution.py:369
  6.7 0.6 copy.12
  7.3 88.4 %shard_map.17 = (f32[2,8,256,256]{3,2,1,0:T(8,128)S(1)}, f32[2,12,256,256]{3,2,1,0:T(8,128)}) custom-call(f32[6,256,256]{2,1,0:T(8,128)S(1)} %bitcast.17, f32[12,256,256]{2,1,0:T(8,128)S(1)} %bitcast.16), custom_call_target="tpu_custom_call" | custom-call | tf_op jit(solution)/shard_map/pallas_call | solution.py:343
  95.8 0.0 copy-start
  95.8 0.1 slice_bitcast_fusion.1
  95.8 0.1 select_maximum_fusion.d_ref
  96.0 27.5 %shard_map.18 = (f32[512,512]{1,0:T(8,128)S(1)}, f32[512,512]{1,0:T(8,128)S(1)}) custom-call(f32[512,512]{1,0:T(8,128)S(1)} %select_maximum_fusion.d_ref), custom_call_target="tpu_custom_call" | custom-call | flops 268435456 | bytes 3145728 | tf_op jit(solution)/shard_map/pallas_call | solution.py:103
  123.5 0.0 copy-start.1
  123.5 1.0 copy-done.1
  124.5 0.0 copy-start.2
  124.5 1.0 copy-done.2
  125.5 0.0 copy-done
  125.5 43.6 %shard_map.19 = f32[36864,128]{1,0:T(8,128)} custom-call(f32[36864,128]{1,0:T(8,128)} %bitcast.18, f32[2,8,256,256]{3,2,1,0:T(8,128)} %copy-done, f32[2,12,256,256]{3,2,1,0:T(8,128)} %get-tuple-element.10.c_ref, f32[512,512]{1,0:T(8,128)} %copy-done.2, f32[512,512]{1,0:T(8,128)} %copy-done.1), custom_call_target="tpu_custom_call" | custom-call | flops 14495514624 | bytes 37748736 | tf_op jit(solution)/shard_map/pallas_call | solution.py:180
Async XLA Ops:
  95.8 29.7 %copy-start = (f32[2,8,256,256]{3,2,1,0:T(8,128)}, f32[2,8,256,256]{3,2,1,0:T(8,128)S(1)}, u32[]{:S(2)}) copy-start(f32[2,8,256,256]{3,2,1,0:T(8,128)S(1)} %get-tuple-element.9.r_ref) | copy-start | bytes 12582916
  123.5 1.0 copy-start.1
  124.5 1.0 copy-start.2
